TPU v7x, 512 devices: a whole 4x4x16 slice. The times are simulated.
512 devices in a mesh: seq: 128 (over z, y, core), ch: 4 (over x).
Axes of the slice: x: 4, y: 4, z: 16, core: 2. Of those that a mesh axis runs over, the one named last changes fastest.
Arguments:
- ingest: bfloat16 [131072, 4096], P('seq', 'ch'), may hold values from -6 to 6
- ingest_count: int32 [128], P('seq'), may hold values from 0 to 1024, as said below
- doc_lengths: int32 [128], replicated, may hold values from 1 to 2048, as said below
- in_weight: bfloat16 [4096, 5120], P('seq', 'ch'), may hold values from -0.09375 to 0.09375
- conv_weight: float32 [4, 5120], P(None, 'ch'), may hold values from -3 to 3
- conv_bias: float32 [5120], P('ch'), may hold values from -3 to 3
Outputs:
- conv_out: bfloat16 [65536, 5120], P('seq', 'ch')
Inputs may be any that keep to these rules, and one draw needn't show every extreme that they name: Device i keeps its valid rows in its first ingest_count[i] slots; the devices before i together hold between i * 512 - 256 and i * 512 + 256 rows, both ends reached in every draw; the first device holds 511 rows, and all devices together hold 65536 rows. `doc_lengths`: the lengths sum to 65536; the first document has exactly 2048 tokens.
All inputs are finite; a program needn't handle non-finite values.
Results may differ from a plain program's by a relative error of at most 0.012.
Values may be sent and summed in bfloat16 or wider, within the bound.
A program may use at most 128 MiB of HBM per device.

v0:
```python
import jax
import jax.numpy as jnp
from jax import lax
from jax.sharding import PartitionSpec as P


def shifted(value, axis, steps):
    count = lax.axis_size(axis)
    initial, last = (max(0, -steps), min(count, count - steps))
    return lax.ppermute(value, axis, [(source, source + steps) for source in range(initial, last)])


def carried_in(value, axis, join, neutral):
    count, mine = (lax.axis_size(axis), lax.axis_index(axis))
    pieces = lax.all_gather(value, axis)
    subtotal = jnp.full_like(value, 0) + jnp.asarray(neutral, value.dtype)

    def turn(position, subtotal):
        longer = join(subtotal, pieces[position])
        return jnp.where(position < mine, longer, subtotal)

    return lax.fori_loop(0, count - 1, turn, subtotal)


def move_rows(ingest, count, offset, first, tokens, extra):
    half = tokens // 2
    slots = ingest.shape[0]
    start = first + tokens - offset - extra
    tail = lax.dynamic_slice_in_dim(ingest, start, half + extra, 0)
    from_left = shifted(tail, "seq", 1)
    from_right = shifted(ingest[:half], "seq", -1)
    next_offset = offset + count
    buffer = jnp.concatenate([from_left, ingest, from_right], axis=0)
    places = first - extra + jnp.arange(tokens + extra, dtype=jnp.int32)
    lead = half + extra
    picks = jnp.where(
        places < offset,
        places - (first - extra),
        jnp.where(
            places < next_offset, lead + places - offset, lead + slots + places - next_offset
        ),
    )
    return jnp.take(buffer, picks.astype(jnp.int32), axis=0)


def body(ingest, ingest_count, doc_lengths, in_weight, conv_weight, conv_bias):
    tokens = ingest.shape[0] // 2
    channels = in_weight.shape[1]
    before = carried_in(
        ingest_count, "seq", lambda earlier, later: earlier + later, jnp.zeros_like(ingest_count)
    )
    offset = before[0]
    count = ingest_count[0]
    first = lax.axis_index("seq") * tokens
    extra = 3
    moved = move_rows(ingest, count, offset, first, tokens, extra)
    features = lax.all_gather(moved, "ch", axis=1, tiled=True)
    window = jnp.dot(
        features,
        lax.all_gather(in_weight, "seq", axis=0, tiled=True),
        preferred_element_type=jnp.float32,
    ).astype(jnp.bfloat16)
    values = window.astype(jnp.float32)
    starts = jnp.cumsum(doc_lengths) - doc_lengths
    places = first - 3 + jnp.arange(tokens + 3, dtype=jnp.int32)
    doc_ids = jnp.sum((places[:, None] >= starts[None, :]).astype(jnp.int32), axis=1) - 1
    here_ids = doc_ids[3:]
    total = jnp.zeros((tokens, channels), jnp.float32) + conv_bias[None, :]
    for lag in range(4):
        earlier = values[3 - lag : 3 - lag + tokens]
        same = (doc_ids[3 - lag : 3 - lag + tokens] == here_ids).astype(jnp.float32)
        total = total + conv_weight[lag][None, :] * earlier * same[:, None]
    return jax.nn.silu(total).astype(jnp.bfloat16)


def solution(mesh):
    placed = (P("seq", "ch"), P("seq"), P(), P("seq", "ch"), P(None, "ch"), P("ch"))
    return jax.shard_map(
        body, mesh=mesh, in_specs=placed, out_specs=P("seq", "ch"), check_vma=False
    )
```

profile of v0, /device:TPU:1, one launch (start us, length us, event | category | flops | bytes accessed | tf_op | source)
XLA Modules:
  0.0 486.9 jit_solution(12569060451620937295)
XLA Ops:
  7.2 1.3 dynamic-slice
  8.5 0.8 dynamic-update-slice
  9.2 30.5 %all-reduce = s32[128]{0:T(128)S(1)} all-reduce(s32[128]{0:T(128)S(1)} %dynamic-update-slice), channel_id=2, replica_groups=mesh['seq'=128,'ch'=4] {'seq'}, use_global_device_ids=true, to_apply=%add | all-reduce | flops 128 | bytes 1024
  39.7 175.2 %while.13 = (s32[]{:T(128)}, s32[1]{0:T(128)}, s32[]{:T(128)}, s32[128,1]{0,1:T(1,128)S(1)}, s32[]{:T(128)}) while((s32[]{:T(128)}, s32[1]{0:T(128)}, s32[]{:T(128)}, s32[128,1]{0,1:T(1,128)S(1)}, s32[]{:T(128)}) %tuple.40), condition=%wide.region_1.2_spmd, body=%wide.region_0.1_spmd.sunk | while | flops 5 | bytes 107 | solution.py:22
  41.1 0.7 constant_dynamic-slice_fusion.3
  42.5 0.7 constant_dynamic-slice_fusion.3
  43.9 0.7 constant_dynamic-slice_fusion.3
  45.3 0.7 constant_dynamic-slice_fusion.3
  46.6 0.7 constant_dynamic-slice_fusion.3
  48.0 0.7 constant_dynamic-slice_fusion.3
  49.4 0.7 constant_dynamic-slice_fusion.3
  50.8 0.7 constant_dynamic-slice_fusion.3
  52.2 0.7 constant_dynamic-slice_fusion.3
  53.5 0.7 constant_dynamic-slice_fusion.3
  54.9 0.7 constant_dynamic-slice_fusion.3
  56.3 0.7 constant_dynamic-slice_fusion.3
  57.7 0.7 constant_dynamic-slice_fusion.3
  59.1 0.7 constant_dynamic-slice_fusion.3
  60.4 0.7 constant_dynamic-slice_fusion.3
  61.8 0.7 constant_dynamic-slice_fusion.3
  63.2 0.7 constant_dynamic-slice_fusion.3
  64.6 0.7 constant_dynamic-slice_fusion.3
  66.0 0.7 constant_dynamic-slice_fusion.3
  67.3 0.7 constant_dynamic-slice_fusion.3
  68.7 0.7 constant_dynamic-slice_fusion.3
  70.1 0.7 constant_dynamic-slice_fusion.3
  71.5 0.7 constant_dynamic-slice_fusion.3
  72.9 0.7 constant_dynamic-slice_fusion.3
  74.2 0.7 constant_dynamic-slice_fusion.3
  75.6 0.7 constant_dynamic-slice_fusion.3
  77.0 0.7 constant_dynamic-slice_fusion.3
  78.4 0.7 constant_dynamic-slice_fusion.3
  79.8 0.7 constant_dynamic-slice_fusion.3
  81.1 0.7 constant_dynamic-slice_fusion.3
  82.5 0.7 constant_dynamic-slice_fusion.3
  83.9 0.7 constant_dynamic-slice_fusion.3
  85.3 0.7 constant_dynamic-slice_fusion.3
  86.7 0.7 constant_dynamic-slice_fusion.3
  88.0 0.7 constant_dynamic-slice_fusion.3
  89.4 0.7 constant_dynamic-slice_fusion.3
  90.8 0.7 constant_dynamic-slice_fusion.3
  92.2 0.7 constant_dynamic-slice_fusion.3
  93.6 0.7 constant_dynamic-slice_fusion.3
  94.9 0.7 constant_dynamic-slice_fusion.3
  96.3 0.7 constant_dynamic-slice_fusion.3
  97.7 0.7 constant_dynamic-slice_fusion.3
  99.1 0.7 constant_dynamic-slice_fusion.3
  100.5 0.7 constant_dynamic-slice_fusion.3
  101.8 0.7 constant_dynamic-slice_fusion.3
  103.2 0.7 constant_dynamic-slice_fusion.3
  215.0 1.2 constant_dynamic-slice_fusion.1
  216.2 7.4 %collective-permute-start = (bf16[259,1024]{1,0:T(8,128)(2,1)S(1)}, bf16[259,1024]{1,0:T(8,128)(2,1)}, u32[]{:S(2)}, u32[]{:S(2)}) collective-permute-start(bf16[259,1024]{1,0:T(8,128)(2,1)S(1)} %constant_dynamic-slice_fusion.1), channel_id=1, source_target_pairs={{0,4},{4,8},{8,12},{12,16},{16,20},{20,24},{24,28},{28,32},{32,36}... | collective-permute-start | bytes 1591304 | tf_op jit(solution)/shard_map/ppermute | solution.py:10
  223.6 1.1 slice.41
  224.7 2.2 collective-permute-start.1
  227.0 8.2 %collective-permute-done.1 = bf16[256,1024]{1,0:T(8,128)(2,1)S(1)} collective-permute-done((bf16[256,1024]{1,0:T(8,128)(2,1)S(1)}, bf16[256,1024]{1,0:T(8,128)(2,1)S(1)}, u32[]{:S(2)}, u32[]{:S(2)}) %collective-permute-start.1) | collective-permute-done | bytes 524320 | tf_op jit(solution)/shard_map/ppermute | solution.py:10
  235.2 0.8 copy-done
  236.0 14.8 %concatenate.3 = bf16[1539,1024]{1,0:T(8,128)(2,1)S(1)} concatenate(bf16[259,1024]{1,0:T(8,128)(2,1)} %collective-permute-done, bf16[1024,1024]{1,0:T(8,128)(2,1)} %param.8, bf16[256,1024]{1,0:T(8,128)(2,1)} %copy-done), dimensions={0} | concatenate | bytes 6303744 | tf_op jit(solution)/shard_map/concatenate | solution.py:33
  250.8 3.4 gather_fusion
  254.1 2.4 broadcast_select_fusion
  256.6 0.7 all-gather.6.cloned.1.call-update
  258.2 52.7 %all-gather.4.cloned.1.call-done = bf16[515,4096]{1,0:T(8,128)(2,1)} async-done(((bf16[515,1024]{1,0:T(8,128)(2,1)}), bf16[515,4096]{1,0:T(8,128)(2,1)}) %all-gather.4.cloned.1.call-update) | async-done | bytes 4218896 | tf_op jit(solution)/shard_map/all_gather | solution.py:57
  310.8 154.9 %all-gather.6.cloned.1.call-done = bf16[4096,1280]{1,0:T(8,128)(2,1)} async-done(((bf16[32,1280]{1,0:T(8,128)(2,1)}), bf16[4096,1280]{1,0:T(8,128)(2,1)}) %all-gather.6.cloned.1.call-update) | async-done | bytes 10485776 | tf_op jit(solution)/shard_map/all_gather | solution.py:60
  465.8 10.9 %fusion = f32[515,1280]{1,0:T(8,128)S(1)} fusion(bf16[515,4096]{1,0:T(8,128)(2,1)} %all-gather.4.cloned.1.call-done, bf16[4096,1280]{1,0:T(8,128)(2,1)} %all-gather.6.cloned.1.call-done), kind=kOutput, calls=%fused_computation.3 | convolution fusion | flops 5401485312 | bytes 17341440 | tf_op jit(solution)/shard_map/dot_general | solution.py:58
  476.7 3.3 multiply_convert_fusion
  (105 shorter events, 54.7 us)
Async XLA Ops:
  6.5 304.3 %all-gather.4.cloned.1.call-start = ((), (), s32[]{:S(2)}) async-start(), calls=%async_computation | async-start | bytes 5324800 | tf_op jit(solution)/shard_map/all_gather | solution.py:57
  216.2 19.8 %collective-permute-start = (bf16[259,1024]{1,0:T(8,128)(2,1)S(1)}, bf16[259,1024]{1,0:T(8,128)(2,1)}, u32[]{:S(2)}, u32[]{:S(2)}) collective-permute-start(bf16[259,1024]{1,0:T(8,128)(2,1)S(1)} %constant_dynamic-slice_fusion.1), channel_id=1, source_target_pairs={{0,4},{4,8},{8,12},{12,16},{16,20},{20,24},{24,28},{28,32},{32,36}... | collective-permute-start | bytes 1591304 | tf_op jit(solution)/shard_map/ppermute | solution.py:10
  224.7 10.5 %collective-permute-start.1 = (bf16[256,1024]{1,0:T(8,128)(2,1)S(1)}, bf16[256,1024]{1,0:T(8,128)(2,1)S(1)}, u32[]{:S(2)}, u32[]{:S(2)}) collective-permute-start(bf16[256,1024]{1,0:T(8,128)(2,1)S(1)} %slice.41), channel_id=1, source_target_pairs={{4,0},{8,4},{12,8},{16,12},{20,16},{24,20},{28,24},{32,28},{36,32}... | collective-permute-start | bytes 1572872 | tf_op jit(solution)/shard_map/ppermute | solution.py:10
  235.2 0.8 copy-start
  254.1 3.2 copy-start.3
  254.1 3.9 copy-start.1
  256.6 209.2 %all-gather.6.cloned.1.call-start = ((), (), s32[]{:S(2)}) async-start(), calls=%async_computation.1 | async-start | bytes 10567680 | tf_op jit(solution)/shard_map/all_gather | solution.py:60
  258.2 218.6 %copy-start.2 = (f32[1280]{0:T(1024)S(1)}, f32[1280]{0:T(1024)}, u32[]{:S(2)}) copy-start(f32[1280]{0:T(1024)} %param.13) | copy-start | bytes 15364
Sparse Core Ops, SparseCore 0:
  256.7 54.0 all-gather.3
  313.9 151.7 all-gather.5
where the time goes:
time: 489 us; the launch traced here: 487 us
  waiting for transfers between devices  217 us (44%)
  local copies, waits for them, and re-layouts  108 us (22%)
  loops' own time  90.8 us (19%)
  blocking collectives  30.5 us (6%)
  between operations  14.2 us (3%)
  matrix products  10.9 us (2%)
  starting transfers between devices  9.63 us (2%)
  other arithmetic  6.33 us (1%)
    all_gather x1, waiting for transfers between devices, body(): lax.all_gather(in_weight, 'seq', axis=0, tiled=True)  155 us
    another operation x1, loops' own time, carried_in(): return lax.fori_loop(0, count - 1, turn, subtotal)  90.8 us
    dynamic_slice x127, local copies, waits for them, and re-layouts, turn(): longer = join(subtotal, pieces[position])  84.4 us
    all_gather x1, waiting for transfers between devices, body(): features = lax.all_gather(moved, 'ch', axis=1, tiled=True)  52.7 us
    unnamed x1, blocking collectives  30.5 us
    concatenate x1, local copies, waits for them, and re-layouts, move_rows(): buffer = jnp.concatenate([from_left, ingest, from_right], axis=0)  14.8 us
    dot_general x1, matrix products, body(): jnp.dot(features, lax.all_gather(in_weight, 'seq', axis=0, tiled=True), p...  10.9 us
  transfers between devices with their start and end apart: 4, of which 3 were waited for; matrix products, arithmetic and copies ran while one was open for 0% of the time, Pallas kernels for 0%

commit v1 on v0

--- a/solution.py
+++ b/solution.py
@@ -54,7 +54,19 @@
     first = lax.axis_index("seq") * tokens
     extra = 3
     moved = move_rows(ingest, count, offset, first, tokens, extra)
-    features = lax.all_gather(moved, "ch", axis=1, tiled=True)
+    ways, here, lap = (lax.axis_size("ch"), lax.axis_index("ch"), moved.shape[1])
+    shape = [n * ways if d == 1 else n for d, n in enumerate(moved.shape)]
+    full = lax.dynamic_update_slice_in_dim(jnp.zeros(shape, moved.dtype), moved, here * lap, axis=1)
+    going_up = going_down = moved
+    for far in range(1, ways // 2 + 1):
+        going_up = lax.ppermute(going_up, "ch", [(d, (d + 1) % ways) for d in range(ways)])
+        full = lax.dynamic_update_slice_in_dim(full, going_up, (here - far) % ways * lap, axis=1)
+        if 2 * far < ways:
+            going_down = lax.ppermute(going_down, "ch", [(d, (d - 1) % ways) for d in range(ways)])
+            full = lax.dynamic_update_slice_in_dim(
+                full, going_down, (here + far) % ways * lap, axis=1
+            )
+    features = full
     window = jnp.dot(
         features,
         lax.all_gather(in_weight, "seq", axis=0, tiled=True),

time: 489 us -> 305 us (0.62)
  the two profiles are of different devices: /device:TPU:1 before, /device:TPU:8 now
where the time goes in v1:
time: 305 us; the launch traced here: 304 us
  local copies, waits for them, and re-layouts  101 us (33%)
  loops' own time  72.9 us (24%)
  waiting for transfers between devices  52.5 us (17%)
  blocking collectives  33.3 us (11%)
  starting transfers between devices  14.8 us (5%)
  between operations  14.3 us (5%)
  matrix products  11 us (4%)
  other arithmetic  4.19 us (1%)
    another operation x1, loops' own time, carried_in(): return lax.fori_loop(0, count - 1, turn, subtotal)  72.9 us
    dynamic_slice x127, local copies, waits for them, and re-layouts, turn(): longer = join(subtotal, pieces[position])  70.7 us
    ppermute x2, waiting for transfers between devices, body(): lax.ppermute(going_up, 'ch', [(d, (d + 1) % ways) for d in range(ways)])  45.2 us
    unnamed x1, blocking collectives  33.3 us
    concatenate x1, local copies, waits for them, and re-layouts, move_rows(): buffer = jnp.concatenate([from_left, ingest, from_right], axis=0)  14.8 us
    dot_general x1, matrix products, body(): jnp.dot(features, lax.all_gather(in_weight, 'seq', axis=0, tiled=True), p...  11 us
    ppermute x2, waiting for transfers between devices, shifted(): lax.ppermute(value, axis, [(source, source + steps) for source in range(i...  6.61 us
  transfers between devices with their start and end apart: 6, of which 3 were waited for; matrix products, arithmetic and copies ran while one was open for 32% of the time, Pallas kernels for 0%

profile of v1, /device:TPU:8, one launch (start us, length us, event | category | flops | bytes accessed | tf_op | source)
XLA Modules:
  0.0 303.5 jit_solution(6760010855145460539)
XLA Ops:
  6.5 0.7 all-gather.3.cloned.1.call-update
  7.9 1.2 dynamic-slice
  9.2 0.7 dynamic-update-slice
  9.8 33.3 %all-reduce = s32[128]{0:T(128)S(1)} all-reduce(s32[128]{0:T(128)S(1)} %dynamic-update-slice), channel_id=2, replica_groups=mesh['seq'=128,'ch'=4] {'seq'}, use_global_device_ids=true, to_apply=%add | all-reduce | flops 128 | bytes 1024
  43.1 143.6 %while.13 = (s32[]{:T(128)}, s32[1]{0:T(128)}, s32[]{:T(128)}, s32[128,1]{0,1:T(1,128)S(1)}, s32[]{:T(128)}) while((s32[]{:T(128)}, s32[1]{0:T(128)}, s32[]{:T(128)}, s32[128,1]{0,1:T(1,128)S(1)}, s32[]{:T(128)}) %tuple.39), condition=%wide.region_1.2_spmd, body=%wide.region_0.1_spmd.sunk | while | flops 5 | bytes 107 | solution.py:22
  44.2 0.6 constant_dynamic-slice_fusion.3
  45.4 0.6 constant_dynamic-slice_fusion.3
  46.5 0.6 constant_dynamic-slice_fusion.3
  47.6 0.6 constant_dynamic-slice_fusion.3
  48.8 0.6 constant_dynamic-slice_fusion.3
  49.9 0.6 constant_dynamic-slice_fusion.3
  51.0 0.6 constant_dynamic-slice_fusion.3
  52.2 0.6 constant_dynamic-slice_fusion.3
  53.3 0.6 constant_dynamic-slice_fusion.3
  54.4 0.6 constant_dynamic-slice_fusion.3
  55.5 0.6 constant_dynamic-slice_fusion.3
  56.7 0.6 constant_dynamic-slice_fusion.3
  57.8 0.6 constant_dynamic-slice_fusion.3
  58.9 0.6 constant_dynamic-slice_fusion.3
  60.1 0.6 constant_dynamic-slice_fusion.3
  61.2 0.6 constant_dynamic-slice_fusion.3
  62.3 0.6 constant_dynamic-slice_fusion.3
  63.5 0.6 constant_dynamic-slice_fusion.3
  64.6 0.6 constant_dynamic-slice_fusion.3
  65.7 0.6 constant_dynamic-slice_fusion.3
  66.9 0.6 constant_dynamic-slice_fusion.3
  68.0 0.6 constant_dynamic-slice_fusion.3
  69.1 0.6 constant_dynamic-slice_fusion.3
  70.2 0.6 constant_dynamic-slice_fusion.3
  71.4 0.6 constant_dynamic-slice_fusion.3
  72.5 0.6 constant_dynamic-slice_fusion.3
  73.6 0.6 constant_dynamic-slice_fusion.3
  74.8 0.6 constant_dynamic-slice_fusion.3
  75.9 0.6 constant_dynamic-slice_fusion.3
  89.5 0.6 constant_dynamic-slice_fusion.3
  92.9 0.6 constant_dynamic-slice_fusion.3
  107.6 0.6 constant_dynamic-slice_fusion.3
  125.6 0.6 constant_dynamic-slice_fusion.3
  142.6 0.6 constant_dynamic-slice_fusion.3
  146.0 0.6 constant_dynamic-slice_fusion.3
  159.6 0.6 constant_dynamic-slice_fusion.3
  163.0 0.6 constant_dynamic-slice_fusion.3
  181.0 0.6 constant_dynamic-slice_fusion.3
  184.4 0.6 constant_dynamic-slice_fusion.3
  186.7 1.2 constant_dynamic-slice_fusion.1
  187.9 1.9 collective-permute-start
  189.8 1.1 slice.41
  190.9 3.6 %collective-permute-start.1 = (bf16[256,1024]{1,0:T(8,128)(2,1)S(1)}, bf16[256,1024]{1,0:T(8,128)(2,1)S(1)}, u32[]{:S(2)}, u32[]{:S(2)}) collective-permute-start(bf16[256,1024]{1,0:T(8,128)(2,1)S(1)} %slice.41), channel_id=1, source_target_pairs={{4,0},{8,4},{12,8},{16,12},{20,16},{24,20},{28,24},{32,28},{36,32}... | collective-permute-start | bytes 1572872 | tf_op jit(solution)/shard_map/ppermute | solution.py:10
  194.6 6.6 %collective-permute-done.1 = bf16[256,1024]{1,0:T(8,128)(2,1)S(1)} collective-permute-done((bf16[256,1024]{1,0:T(8,128)(2,1)S(1)}, bf16[256,1024]{1,0:T(8,128)(2,1)S(1)}, u32[]{:S(2)}, u32[]{:S(2)}) %collective-permute-start.1) | collective-permute-done | bytes 524320 | tf_op jit(solution)/shard_map/ppermute | solution.py:10
  201.2 0.8 copy-done.2
  202.0 14.8 %concatenate.3 = bf16[1539,1024]{1,0:T(8,128)(2,1)S(1)} concatenate(bf16[259,1024]{1,0:T(8,128)(2,1)} %collective-permute-done, bf16[1024,1024]{1,0:T(8,128)(2,1)} %param.8, bf16[256,1024]{1,0:T(8,128)(2,1)} %copy-done.2), dimensions={0} | concatenate | bytes 6303744 | tf_op jit(solution)/shard_map/concatenate | solution.py:33
  216.8 3.4 %gather_fusion = bf16[515,1024]{1,0:T(8,128)(2,1)} fusion(bf16[1539,1024]{1,0:T(8,128)(2,1)S(1)} %concatenate.3, s32[1024]{0:T(1024)S(1)} %pad_clamp_fusion), kind=kCustom, calls=%fused_computation | custom fusion | bytes 2111500 | tf_op jit(solution)/shard_map/jit(_take)/gather | solution.py:43
  220.7 0.7 copy-done
  221.7 2.1 copy-done.1
  223.8 3.4 %collective-permute-start.2 = (bf16[515,1024]{1,0:T(8,128)(2,1)S(1)}, bf16[515,1024]{1,0:T(8,128)(2,1)S(1)}, u32[]{:S(2)}, u32[]{:S(2)}) collective-permute-start(bf16[515,1024]{1,0:T(8,128)(2,1)S(1)} %get-tuple-element.98), channel_id=1, source_target_pairs={{0,1},{1,2},{2,3},{3,0},{4,5},{5,6},{6,7},{7,4},{8,9},{9,10},{10,1... | collective-permute-start | bytes 3164168 | tf_op jit(solution)/shard_map/ppermute | solution.py:62
  227.2 3.6 %collective-permute-start.3 = (bf16[515,1024]{1,0:T(8,128)(2,1)S(1)}, bf16[515,1024]{1,0:T(8,128)(2,1)S(1)}, u32[]{:S(2)}, u32[]{:S(2)}) collective-permute-start(bf16[515,1024]{1,0:T(8,128)(2,1)S(1)} %get-tuple-element.98), channel_id=1, source_target_pairs={{0,3},{1,0},{2,1},{3,2},{4,7},{5,4},{6,5},{7,6},{8,11},{9,8},{10,9... | collective-permute-start | bytes 3164168 | tf_op jit(solution)/shard_map/ppermute | solution.py:65
  231.3 21.7 %collective-permute-done.2 = bf16[515,1024]{1,0:T(8,128)(2,1)S(1)} collective-permute-done((bf16[515,1024]{1,0:T(8,128)(2,1)S(1)}, bf16[515,1024]{1,0:T(8,128)(2,1)S(1)}, u32[]{:S(2)}, u32[]{:S(2)}) %collective-permute-start.2) | collective-permute-done | bytes 1054752 | tf_op jit(solution)/shard_map/ppermute | solution.py:62
  253.0 2.2 collective-permute-start.4
  255.6 1.1 constant_dynamic-update-slice_fusion.2
  256.7 1.1 constant_dynamic-update-slice_fusion.1
  257.8 23.6 %collective-permute-done.4 = bf16[515,1024]{1,0:T(8,128)(2,1)S(1)} collective-permute-done((bf16[515,1024]{1,0:T(8,128)(2,1)S(1)}, bf16[515,1024]{1,0:T(8,128)(2,1)S(1)}, u32[]{:S(2)}, u32[]{:S(2)}) %collective-permute-start.4) | collective-permute-done | bytes 1054752 | tf_op jit(solution)/shard_map/ppermute | solution.py:62
  281.4 1.1 constant_dynamic-update-slice_fusion
  282.4 11.0 %fusion = f32[515,1280]{1,0:T(8,128)S(1)} fusion(bf16[515,4096]{1,0:T(8,128)(2,1)} %constant_dynamic-update-slice_fusion, bf16[4096,1280]{1,0:T(8,128)(2,1)} %all-gather.3.cloned.1.call-done), kind=kOutput, calls=%fused_computation.3 | convolution fusion | flops 5401485312 | bytes 17341440 | tf_op jit(solution)/shard_map/dot_general | solution.py:70
  293.4 3.3 %multiply_convert_fusion = bf16[512,1280]{1,0:T(8,128)(2,1)} fusion(f32[515,1280]{1,0:T(8,128)S(1)} %fusion, f32[512]{0:T(512)S(1)} %get-tuple-element.101, f32[1280]{0:T(1024)S(1)} %get-tuple-element.87, f32[512]{0:T(512)S(1)} %get-tuple-element.100, f32[1280]{0:T(1024)S(1)} %get-tuple-element.88, f32[512]{0:T(512)S(1)} %get-tuple-element.99, ...), kind=kLoop, calls=%fused_computation.15 | loop fusion | flops 10485760 | bytes 11828224 | tf_op jit(solution)/shard_map/convert_element_type | solution.py:85
  (116 shorter events, 50.6 us)
Async XLA Ops:
  6.5 275.9 %all-gather.3.cloned.1.call-start = ((), (), s32[]{:S(2)}) async-start(), calls=%async_computation | async-start | bytes 10567680 | tf_op jit(solution)/shard_map/all_gather | solution.py:72
  187.9 14.1 %collective-permute-start = (bf16[259,1024]{1,0:T(8,128)(2,1)S(1)}, bf16[259,1024]{1,0:T(8,128)(2,1)}, u32[]{:S(2)}, u32[]{:S(2)}) collective-permute-start(bf16[259,1024]{1,0:T(8,128)(2,1)S(1)} %constant_dynamic-slice_fusion.1), channel_id=1, source_target_pairs={{0,4},{4,8},{8,12},{12,16},{16,20},{20,24},{24,28},{28,32},{32,36}... | collective-permute-start | bytes 1591304 | tf_op jit(solution)/shard_map/ppermute | solution.py:10
  190.9 10.3 %collective-permute-start.1 = (bf16[256,1024]{1,0:T(8,128)(2,1)S(1)}, bf16[256,1024]{1,0:T(8,128)(2,1)S(1)}, u32[]{:S(2)}, u32[]{:S(2)}) collective-permute-start(bf16[256,1024]{1,0:T(8,128)(2,1)S(1)} %slice.41), channel_id=1, source_target_pairs={{4,0},{8,4},{12,8},{16,12},{20,16},{24,20},{28,24},{32,28},{36,32}... | collective-permute-start | bytes 1572872 | tf_op jit(solution)/shard_map/ppermute | solution.py:10
  201.2 0.8 copy-start.2
  220.2 1.2 copy-start
  221.4 9.5 %copy-start.5 = (s32[128]{0:T(128)S(1)}, s32[128]{0:T(128)}, u32[]{:S(2)}) copy-start(s32[128]{0:T(128)} %param.10) | copy-start | bytes 1540
  221.4 34.0 %copy-start.3 = (f32[4,1280]{1,0:T(4,128)S(1)}, f32[4,1280]{1,0:T(4,128)}, u32[]{:S(2)}) copy-start(f32[4,1280]{1,0:T(4,128)} %param.12) | copy-start | bytes 61444
  221.7 2.1 copy-start.1
  223.8 29.2 %collective-permute-start.2 = (bf16[515,1024]{1,0:T(8,128)(2,1)S(1)}, bf16[515,1024]{1,0:T(8,128)(2,1)S(1)}, u32[]{:S(2)}, u32[]{:S(2)}) collective-permute-start(bf16[515,1024]{1,0:T(8,128)(2,1)S(1)} %get-tuple-element.98), channel_id=1, source_target_pairs={{0,1},{1,2},{2,3},{3,0},{4,5},{5,6},{6,7},{7,4},{8,9},{9,10},{10,1... | collective-permute-start | bytes 3164168 | tf_op jit(solution)/shard_map/ppermute | solution.py:62
  227.2 29.5 %collective-permute-start.3 = (bf16[515,1024]{1,0:T(8,128)(2,1)S(1)}, bf16[515,1024]{1,0:T(8,128)(2,1)S(1)}, u32[]{:S(2)}, u32[]{:S(2)}) collective-permute-start(bf16[515,1024]{1,0:T(8,128)(2,1)S(1)} %get-tuple-element.98), channel_id=1, source_target_pairs={{0,3},{1,0},{2,1},{3,2},{4,7},{5,4},{6,5},{7,6},{8,11},{9,8},{10,9... | collective-permute-start | bytes 3164168 | tf_op jit(solution)/shard_map/ppermute | solution.py:65
  253.0 28.4 %collective-permute-start.4 = (bf16[515,1024]{1,0:T(8,128)(2,1)S(1)}, bf16[515,1024]{1,0:T(8,128)(2,1)S(1)}, u32[]{:S(2)}, u32[]{:S(2)}) collective-permute-start(bf16[515,1024]{1,0:T(8,128)(2,1)S(1)} %collective-permute-done.2), channel_id=1, source_target_pairs={{0,1},{1,2},{2,3},{3,0},{4,5},{5,6},{6,7},{7,4},{8,9},{9,10},{10,1... | collective-permute-start | bytes 3164168 | tf_op jit(solution)/shard_map/ppermute | solution.py:62
  282.4 11.0 %copy-start.4 = (f32[1280]{0:T(1024)S(1)}, f32[1280]{0:T(1024)}, u32[]{:S(2)}) copy-start(f32[1280]{0:T(1024)} %param.13) | copy-start | bytes 15364
Sparse Core Ops, SparseCore 0:
  10.5 152.7 all-gather.2
